TPU v7x, 128 devices: a whole 4x4x4 slice. The times are simulated.
128 devices in a mesh: gx: 8 (over z, core), gy: 8 (over y, x_lo), ta: 2 (over x_hi).
Axes of the slice: x: 4 (x_hi: 2, x_lo: 2; x = x_hi * 2 + x_lo), y: 4, z: 4, core: 2. Of those that a mesh axis runs over, the one named last changes fastest.
Arguments:
- elevations: float32 [1024, 512, 1024], P('gx', 'gy', 'ta'), may hold values from -6 to 6
- time_basis: float32 [1024, 32], P('ta'), may hold values from -0.1875 to 0.1875
- north_basis: float32 [512, 32], P('gy'), may hold values from -0.25 to 0.25
- east_basis: float32 [1024, 32], P('gx'), may hold values from -0.1875 to 0.1875
Outputs:
- core_unfolded: float32 [32, 1024], P(None, ('gx', 'gy', 'ta'))
- gram_matrix: float32 [1024, 1024], P(('gx', 'gy', 'ta'))
All inputs are finite; a program needn't handle non-finite values.
Results may differ from a plain program's by a relative error of at most 0.00009.
Values sent between devices are 32-bit elements; how exact they have to be, the bound alone decides.
A program may use at most 64 MiB of HBM per device.

v0:
```python
import jax
import jax.numpy as jnp
from jax import lax
from jax.sharding import PartitionSpec as P


def shards(elevations, time_basis, north_basis, east_basis):
    highest = lax.Precision.HIGHEST
    east_rows, north_rows, time_rows = elevations.shape
    rank_size = time_basis.shape[1]
    flattened = elevations.reshape(east_rows * north_rows, time_rows)
    time_mode = jnp.dot(flattened, time_basis, precision=highest).reshape(
        east_rows, north_rows, rank_size
    )
    partial_core = jnp.einsum("yp,xyq->xpq", north_basis, time_mode, precision=highest)
    partial_core = partial_core.reshape(east_rows, rank_size * rank_size)
    inverse_count = 1.0 / (rank_size * rank_size)
    spread = lax.axis_size(("gy", "ta"))
    complete = lax.psum_scatter(partial_core, ("gy", "ta"), scatter_dimension=0, tiled=True)
    row_share = east_rows // spread
    local_basis = lax.dynamic_slice_in_dim(
        east_basis, lax.axis_index(("gy", "ta")) * row_share, row_share, 0
    )
    core_terms = jnp.dot(local_basis.T, complete, precision=highest)
    core_unfolded = lax.psum_scatter(
        core_terms, ("gx", "gy", "ta"), scatter_dimension=1, tiled=True
    )
    gram_matrix = (
        jnp.einsum(
            "ac,bc->ab",
            complete,
            lax.all_gather(complete, ("gx", "gy", "ta"), axis=0, tiled=True),
            precision=highest,
        )
        * inverse_count
    )
    return (core_unfolded, gram_matrix)


def solution(mesh):
    in_specs = (P("gx", "gy", "ta"), P("ta", None), P("gy", None), P("gx", None))
    out_specs = (P(None, ("gx", "gy", "ta")), P(("gx", "gy", "ta"), None))
    return jax.shard_map(shards, mesh=mesh, in_specs=in_specs, out_specs=out_specs, check_vma=False)
```

profile of v0, /device:TPU:1, one launch (start us, length us, event | category | flops | bytes accessed | tf_op | source)
XLA Modules:
  0.0 584.5 jit_solution(1927930817829870033)
XLA Ops:
  7.2 0.0 copy-start
  7.2 0.0 copy-start.1
  7.2 0.0 reduce-scatter.4.cloned.1.call-start
  7.2 0.8 copy-done
  8.0 23.4 %fusion.5 = f32[128,64,32]{1,2,0:T(8,128)S(1)} fusion(f32[128,64,512]{2,1,0:T(8,128)} %param.4, f32[512,32]{0,1:T(8,128)S(1)} %copy-done), kind=kOutput, calls=%fused_computation.4 | convolution fusion | flops 1610612736 | bytes 17891328 | tf_op jit(solution)/shard_map/dot_general | solution.py:12
  31.4 0.0 copy-done.1
  31.4 0.0 copy-start.2
  31.4 3.3 fusion.2
  34.7 0.3 copy.8
  35.0 1.0 copy.10
  36.0 0.0 reduce-scatter.4.cloned.1.call-update
  36.0 0.0 all-reduce.3.cloned.1.call-start
  36.1 69.0 %reduce-scatter.4.cloned.1.call-done = f32[8,1024]{1,0:T(8,128)} async-done(((f32[128,1024]{1,0:T(8,128)}), f32[8,1024]{1,0:T(8,128)}) %reduce-scatter.4.cloned.1.call-update) | async-done | bytes 32784
  105.1 0.0 copy-done.2
  105.1 2.6 fusion.8
  107.7 0.0 all-reduce.3.cloned.1.call-update
  107.7 0.2 all-gather.2.cloned.1.call-start
  107.9 0.5 all-gather.2.cloned.1.call-update
  108.4 156.1 %all-reduce.3.cloned.1.call-done = f32[32,1024]{0,1:T(8,128)} async-done(((f32[32,1024]{0,1:T(8,128)}), f32[32,1024]{0,1:T(8,128)}) %all-reduce.3.cloned.1.call-update) | async-done | bytes 131088
  264.5 1.3 constant_dynamic-slice_fusion
  265.8 305.9 %all-gather.2.cloned.1.call-done = f32[1024,1024]{1,0:T(8,128)} async-done(((f32[8,1024]{1,0:T(8,128)}), f32[1024,1024]{1,0:T(8,128)}) %all-gather.2.cloned.1.call-update) | async-done | bytes 4194320 | tf_op jit(solution)/shard_map/all_gather | solution.py:32
  571.7 6.3 %convolution_multiply_fusion = f32[8,1024]{1,0:T(8,128)} fusion(f32[8,1024]{1,0:T(8,128)} %reduce-scatter.4.cloned.1.call-done, f32[1024,1024]{1,0:T(8,128)} %all-gather.2.cloned.1.call-done), kind=kOutput, calls=%fused_computation.3 | convolution fusion | flops 100671488 | bytes 4259840 | tf_op jit(solution)/shard_map/ac,bc->ab/dot_general | solution.py:29
Async XLA Ops:
  7.2 0.8 copy-start
  7.2 24.2 %copy-start.1 = (f32[64,32]{0,1:T(8,128)S(1)}, f32[64,32]{0,1:T(8,128)}, u32[]{:S(2)}) copy-start(f32[64,32]{0,1:T(8,128)} %param.6) | copy-start | bytes 24580
  7.2 97.9 %reduce-scatter.4.cloned.1.call-start = ((), (), s32[]{:S(2)}) async-start(), calls=%async_computation.2 | async-start | bytes 557056
  31.4 73.7 %copy-start.2 = (f32[128,32]{0,1:T(8,128)S(1)}, f32[128,32]{0,1:T(8,128)}, u32[]{:S(2)}) copy-start(f32[128,32]{0,1:T(8,128)} %param.7) | copy-start | bytes 49156
  36.0 228.5 %all-reduce.3.cloned.1.call-start = ((), (), s32[]{:S(2)}) async-start(), calls=%async_computation.3 | async-start | bytes 1048576
  107.7 464.0 %all-gather.2.cloned.1.call-start = ((), (), s32[]{:S(2)}) async-start(), calls=%async_computation.1 | async-start | bytes 4227072 | tf_op jit(solution)/shard_map/all_gather | solution.py:32
Sparse Core Ops, SparseCore 0:
  36.2 68.8 reduce-scatter.3
  110.6 153.9 all-reduce.2
  266.2 305.4 all-gather.1
where the time goes:
time: 585 us; the launch traced here: 584 us
  waiting for transfers between devices  531 us (91%)
  matrix products  35.5 us (6%)
  between operations  13.8 us (2%)
    all_gather x1, waiting for transfers between devices, shards(): lax.all_gather(complete, ('gx', 'gy', 'ta'), axis=0, tiled=True)  306 us
    unnamed x5, waiting for transfers between devices  226 us
    dot_general x1, matrix products, shards(): jnp.dot(flattened, time_basis, precision=highest)  23.4 us
  transfers between devices with their start and end apart: 3, of which 3 were waited for; matrix products, arithmetic and copies ran while one was open for 0% of the time, Pallas kernels for 0%

commit v1 on v0

v1 whole, which is shorter than its diff:
```python
import functools

import jax
import jax.numpy as jnp
from jax import lax
from jax.experimental import pallas as pl
from jax.experimental.pallas import tpu as pltpu
from jax.sharding import PartitionSpec as P

F32 = jnp.float32
BF16 = jnp.bfloat16
MESH = pl.DeviceIdType.MESH
NN = (((1,), (0,)), ((), ()))
NT = (((1,), (1,)), ((), ()))
RING = (0, 1, 3, 2)
CHUNKS = 4
STEP = 8 // CHUNKS
ROUNDS = ((0, 1), (1, 2), (3, 1))
LEGS = ((0, 3), (3, 1))


def split(values):
    high = values.astype(BF16)
    return high, (values - high.astype(F32)).astype(BF16)


def dot(a, b, dims):
    return lax.dot_general(a, b, dims, preferred_element_type=F32)


def exchange(values, lane, unit, stages):
    for s in stages:
        low = (lane // (unit * s)) % 2 == 0
        out = list(values)
        for a in range(len(values)):
            if a & s:
                continue
            out[a] = jnp.where(low, values[a], pltpu.roll(values[a + s], unit * s, 1))
            out[a + s] = jnp.where(low, pltpu.roll(values[a], 128 - unit * s, 1), values[a + s])
        values = out
    return values


def kernel(
    elev, time_t, north_t, east_t, core_out, gram_out,
    slab, time_v, north_v, basis, send1, recv1, mid1, last1, send_last, recv_last,
    blocks, twin, easts, core_part, core_twin, send2, recv2, mid2, last2,
    slab_sem, small_sem, send1_sem, recv1_sem, mid1_sem, last1_sem, direct_send, direct_recv,
    block_send, block_recv, east_send, east_recv, core_send, core_recv,
    send2_sem, recv2_sem, mid2_sem, last2_sem,
):
    gx, gy, ta = lax.axis_index("gx"), lax.axis_index("gy"), lax.axis_index("ta")
    z, core = gx // 2, gx % 2
    y, x = gy // 2, ta * 2 + gy % 2

    def slab_copy(c):
        part = pl.ds(c * STEP, STEP)
        return pltpu.make_async_copy(elev.at[:, part], slab.at[:, part], slab_sem.at[c])

    small = [
        pltpu.make_async_copy(time_t, time_v, small_sem.at[0]),
        pltpu.make_async_copy(north_t, north_v, small_sem.at[1]),
        pltpu.make_async_copy(east_t, easts.at[0], small_sem.at[2]),
    ]
    for copy in small:
        copy.start()
    for c in range(2):
        slab_copy(c).start()

    plane, along_x, along_y, ring, across = [], [], [], [], []
    for slot in range(1, 16):
        y2, x2 = (y + slot // 4) % 4, (x + slot % 4) % 4
        plane.append((slot, (gx, y2 * 2 + x2 % 2, x2 // 2), y2, x2))
    for slot in range(1, 4):
        along_x.append((slot, plane[slot - 1][1], plane[slot - 1][3]))
        along_y.append((slot, plane[slot * 4 - 1][1], plane[slot * 4 - 1][2]))
        ring.append((slot, (((z + RING[slot]) % 4) * 2 + core, gy, ta)))
    for slot in range(4):
        x2 = (x + slot) % 4
        across.append((slot, (z * 2 + 1 - core, y * 2 + x2 % 2, x2 // 2), x2))
    other = across[0][1]
    barrier = pltpu.get_barrier_semaphore()
    for peer in plane + ring + across:
        pl.semaphore_signal(barrier, inc=1, device_id=peer[1], device_id_type=MESH)

    first_leg, second_leg = (along_x, along_y), (along_y, along_x)
    first_at, second_at = (x, y), (y, x)

    for copy in small:
        copy.wait()
    time_high, time_low = split(time_v[...])
    time_both = jnp.concatenate([time_high, time_low], 0)
    time_wide = time_high.astype(F32).T.astype(BF16)
    lane = lax.broadcasted_iota(jnp.int32, (32, 128), 1)

    def make_basis():
        row = lax.broadcasted_iota(jnp.int32, (32, 128), 0)
        spread = jnp.where(4 * ((lane % 32) // 4) + lane // 32 == row, 1.0, 0.0).astype(BF16)
        lane64 = lax.broadcasted_iota(jnp.int32, (64, 128), 1)
        for h, part in enumerate(split(north_v[...].T)):
            wide = dot(part, spread, NN)
            for x4 in range(4):
                own = jnp.where(lane64 % 4 == x4, wide, 0.0).astype(BF16)
                basis[pl.ds(x4 * 64, 64), pl.ds(h * 128, 128)] = own

    def over_time(g, b):
        high, low = split(slab[b, g])
        t = dot(time_both, high, NT)
        return t[:32] + t[32:] + dot(low, time_wide, NN).T

    def over_y(terms):
        high, low = zip(*[split(t) for t in terms])
        r = dot(jnp.concatenate(high, 0), basis[...], NN)
        r = r[:, :128] + r[:, 128:] + dot(jnp.concatenate(low, 0), basis[:, :128], NN)
        return exchange([r[32 * b : 32 * b + 32] for b in range(4)], lane, 32, (2, 1))

    def remote(src, dst, send_sem, recv_sem, device):
        return pltpu.make_async_remote_copy(
            src_ref=src, dst_ref=dst, send_sem=send_sem, recv_sem=recv_sem, device_id=device, device_id_type=MESH
        )

    def await_bytes(ref, sem):
        pltpu.make_async_copy(ref, ref, sem).wait()

    def finish(c, terms):
        for h in range(STEP):
            tiles = over_y(terms[h])
            for pg in range(4):
                for qg in range(4):
                    at = (qg % 2) * 2 + qg // 2
                    f, s = (at, pg) if h == 0 else (pg, at)
                    tile = tiles[pg][qg * 8 : qg * 8 + 8]
                    if c == CHUNKS - 1:
                        send_last[pg, at, h] = tile
                    else:
                        send1[c, h, f, s] = tile
        if c == 0:
            pl.semaphore_wait(barrier, 22)
        if c == CHUNKS - 1:
            for slot, device, y2, x2 in plane:
                remote(send_last.at[y2, x2], recv_last.at[slot], direct_send, direct_recv, device).start()
            return
        for h in range(2):
            for slot, device, at in first_leg[h]:
                remote(
                    send1.at[c, h, at], recv1.at[c, h, slot], send1_sem.at[c], recv1_sem.at[c], device
                ).start()

    def east_copy(slot, device):
        return remote(easts.at[0], easts.at[slot], east_send, east_recv, device)

    held = None
    for c in range(CHUNKS):
        slab_copy(c).wait()
        if c + 2 < CHUNKS:
            slab_copy(c + 2).start()
        terms = [[over_time(c * STEP + k, b) for b in range(4)] for k in range(STEP)]
        if c == 0:
            make_basis()
        else:
            finish(c - 1, held)
            if c == 1:
                for peer in ring:
                    east_copy(*peer).start()
        held = terms
    finish(CHUNKS - 1, held)

    for c in range(CHUNKS - 1):
        await_bytes(recv1.at[c, :, pl.ds(1, 3)], recv1_sem.at[c])
    for h in range(2):
        for c in range(CHUNKS - 1):
            total = send1[c, h, first_at[h]]
            for slot in range(1, 4):
                total = total + recv1[c, h, slot]
            for k in range(4):
                mid1[h, k, c] = total[k]
        for slot, device, at in second_leg[h]:
            remote(mid1.at[h, at], last1.at[h, slot], mid1_sem, last1_sem, device).start()
    tiles = []
    await_bytes(last1.at[:, pl.ds(1, 3)], last1_sem)
    for c in range(CHUNKS - 1):
        for h in range(2):
            total = mid1[h, second_at[h], c]
            for slot in range(1, 4):
                total = total + last1[h, slot, c]
            tiles.append(total)
    await_bytes(recv_last.at[pl.ds(1, 15)], direct_recv)
    for h in range(2):
        total = send_last[y, x, h]
        for slot in range(1, 16):
            total = total + recv_last[slot, h]
        tiles.append(total)
    lane8 = lax.broadcasted_iota(jnp.int32, (8, 128), 1)
    tiles = exchange(tiles, lane8, 4, (4, 2, 1))
    for i in range(8):
        blocks[0, pl.ds(i * 8, 8), :] = tiles[i]

    def block_copy(slot, device):
        return remote(blocks.at[0], blocks.at[slot], block_send.at[slot], block_recv.at[slot], device)

    twin_copy = remote(blocks.at[0], twin, block_send.at[0], block_recv.at[0], other)
    for peer in ring[::-1]:
        block_copy(*peer).start()
    twin_copy.start()

    def left_side(block):
        high, low = split(block.T)
        return jnp.concatenate([high, high, low], 1)

    lefts = [left_side(jnp.concatenate(tiles, 0))]
    for r, (start, count) in enumerate(ROUNDS):
        for slot in range(start, start + count):
            if slot > 0:
                block_copy(*ring[slot - 1]).wait_recv()
            high, low = split(blocks[slot])
            right = jnp.concatenate([high, low, high], 0)
            for h in range(2):
                if len(lefts) == h:
                    twin_copy.wait_recv()
                    lefts.append(left_side(twin[...]))
                part = dot(lefts[h], right, NN)
                for index in range(16):
                    pg, qg = index // 4, index % 4
                    at = (qg % 2) * 2 + qg // 2
                    f, s = (at, pg) if h == 0 else (pg, at)
                    send2[h, f, slot, s] = part[index * 8 : index * 8 + 8]
        slots = pl.ds(start, count)
        for h in range(2):
            for slot, device, at in first_leg[h]:
                remote(
                    send2.at[h, at, slots], recv2.at[h, slot, slots], send2_sem.at[r], recv2_sem.at[r], device
                ).start()

    await_bytes(easts.at[pl.ds(1, 3)], east_recv)
    rows = [
        jnp.concatenate(
            [blocks[slot, pl.ds(pl.multiple_of(i * 8, 8), 8), :] for i in (gx, z * 2 + 1 - core)], 0
        )
        for slot in range(4)
    ]
    core_sum = lax.dot_general(
        jnp.concatenate(rows, 1),
        jnp.concatenate([easts[slot] for slot in range(4)], 1),
        NT,
        precision=lax.Precision.HIGHEST,
        preferred_element_type=F32,
    )
    core_part[...] = jnp.zeros((8, 128), F32)
    core_part[:, :32] = core_sum[8:]
    core_copy = remote(core_part, core_twin, core_send, core_recv, other)
    core_copy.start()

    done = 0
    for leg, (start, count) in enumerate(LEGS):
        while done < len(ROUNDS) and ROUNDS[done][0] < start + count:
            await_bytes(recv2.at[:, pl.ds(1, 3), pl.ds(*ROUNDS[done])], recv2_sem.at[done])
            done += 1
        part = pl.ds(start, count)
        for h in range(2):
            for pair in range(start, start + count):
                total = send2[h, first_at[h], pair]
                for slot in range(1, 4):
                    total = total + recv2[h, slot, pair]
                for k in range(4):
                    mid2[h, k, pair] = total[k]
            for slot, device, at in (along_y, across)[h]:
                remote(
                    mid2.at[h, at, part], last2.at[h, slot, part], mid2_sem.at[leg, h], last2_sem.at[leg, h], device
                ).start()

    core_copy.wait_recv()
    core_out[...] = core_sum[:8] + core_twin[:, :32]

    inverse_count = 1.0 / 1024.0

    def final(slot, c, total):
        at = (((z + 4 - RING[slot]) % 4) * 2 + c) * 128
        gram_out[:, pl.ds(pl.multiple_of(at, 128), 128)] = total * inverse_count

    for leg, (start, count) in enumerate(LEGS):
        part = pl.ds(start, count)
        await_bytes(last2.at[0, pl.ds(1, 3), part], last2_sem.at[leg, 0])
        for slot in range(start, start + count):
            total = mid2[0, y, slot]
            for peer in range(1, 4):
                total = total + last2[0, peer, slot]
            final(slot, core, total)
        await_bytes(last2.at[1, :, part], last2_sem.at[leg, 1])
        for slot in range(start, start + count):
            total = last2[1, 0, slot]
            for peer in range(1, 4):
                total = total + last2[1, peer, slot]
            final(slot, 1 - core, total)

    for c in range(CHUNKS - 1):
        await_bytes(recv1.at[c, :, pl.ds(1, 3)], send1_sem.at[c])
    await_bytes(last1.at[:, pl.ds(1, 3)], mid1_sem)
    await_bytes(recv_last.at[pl.ds(1, 15)], direct_send)
    await_bytes(easts.at[pl.ds(1, 3)], east_send)
    for peer in ring:
        block_copy(*peer).wait_send()
    twin_copy.wait_send()
    core_copy.wait_send()
    for r, part in enumerate(ROUNDS):
        await_bytes(recv2.at[:, pl.ds(1, 3), pl.ds(*part)], send2_sem.at[r])
    for leg, (start, count) in enumerate(LEGS):
        await_bytes(last2.at[0, pl.ds(1, 3), pl.ds(start, count)], mid2_sem.at[leg, 0])
        await_bytes(last2.at[1, :, pl.ds(start, count)], mid2_sem.at[leg, 1])


def hand_over(core_in, gram_in, core_out, gram_out, sem):
    copies = [
        pltpu.make_async_copy(core_in, core_out, sem.at[0]),
        pltpu.make_async_copy(gram_in, gram_out, sem.at[1]),
    ]
    for copy in copies:
        copy.start()
    for copy in copies:
        copy.wait()


def shards(elevations, time_basis, north_basis, east_basis):
    dma = pltpu.SemaphoreType.DMA
    shapes = ((8, 32), (8, 1024))
    far = pl.BlockSpec(memory_space=pltpu.HBM)
    near = pl.BlockSpec(memory_space=pltpu.VMEM)
    legs = CHUNKS - 1
    core_t, gram = pl.pallas_call(
        kernel,
        out_shape=tuple(pltpu.VMEM(shape, F32) for shape in shapes),
        in_specs=[far] * 4,
        out_specs=(near, near),
        scratch_shapes=[
            pltpu.VMEM((4, 8, 256, 512), F32),
            pltpu.VMEM((32, 512), F32),
            pltpu.VMEM((32, 64), F32),
            pltpu.VMEM((256, 256), BF16),
            pltpu.VMEM((legs, 2, 4, 4, 8, 128), F32),
            pltpu.VMEM((legs, 2, 4, 4, 8, 128), F32),
            pltpu.VMEM((2, 4, legs, 8, 128), F32),
            pltpu.VMEM((2, 4, legs, 8, 128), F32),
            pltpu.VMEM((4, 4, STEP, 8, 128), F32),
            pltpu.VMEM((16, STEP, 8, 128), F32),
            pltpu.VMEM((4, 64, 128), F32),
            pltpu.VMEM((64, 128), F32),
            pltpu.VMEM((4, 32, 128), F32),
            pltpu.VMEM((8, 128), F32),
            pltpu.VMEM((8, 128), F32),
            pltpu.VMEM((2, 4, 4, 4, 8, 128), F32),
            pltpu.VMEM((2, 4, 4, 4, 8, 128), F32),
            pltpu.VMEM((2, 4, 4, 8, 128), F32),
            pltpu.VMEM((2, 4, 4, 8, 128), F32),
            dma((CHUNKS,)),
            dma((3,)),
            dma((legs,)),
            dma((legs,)),
            dma,
            dma,
            dma,
            dma,
            dma((4,)),
            dma((4,)),
            dma,
            dma,
            dma,
            dma,
            dma((3,)),
            dma((3,)),
            dma((2, 2)),
            dma((2, 2)),
        ],
        compiler_params=pltpu.CompilerParams(
            collective_id=0, has_side_effects=True, vmem_limit_bytes=59 << 20
        ),
    )(elevations.reshape(4, 8, 256, 512), time_basis.T, north_basis.T, east_basis.T)
    core_t, gram = pl.pallas_call(
        hand_over,
        out_shape=tuple(jax.ShapeDtypeStruct(shape, F32) for shape in shapes),
        in_specs=[near, near],
        out_specs=(far, far),
        scratch_shapes=[dma((2,))],
        compiler_params=pltpu.CompilerParams(vmem_limit_bytes=59 << 20),
    )(pltpu.with_memory_space_constraint(core_t, pltpu.VMEM), pltpu.with_memory_space_constraint(gram, pltpu.VMEM))
    return core_t.T, gram


def solution(mesh):
    in_specs = (P("gx", "gy", "ta"), P("ta", None), P("gy", None), P("gx", None))
    out_specs = (P(None, ("gx", "gy", "ta")), P(("gx", "gy", "ta"), None))
    return jax.shard_map(shards, mesh=mesh, in_specs=in_specs, out_specs=out_specs, check_vma=False)
```

time: 585 us -> 35.3 us (0.06)
  waiting for transfers between devices: 531 us -> 0 us
  matrix products: 35.5 us -> 0 us
  Pallas kernels: 0 us -> 34.5 us
  between operations: 13.8 us -> 0.64 us
    all_gather x1 -> x0, waiting for transfers between devices: 306 us -> none  [shards(): lax.all_gather(complete, ('gx', 'gy', 'ta'), axis=0, tiled=True)]
    unnamed x5 -> x0, waiting for transfers between devices: 226 us -> none
    dot_general x4 -> x0, matrix products: 35.5 us -> none  [the longest x1 23.4 us: shards(): jnp.dot(flattened, time_basis, precision=highest)]
    pallas_call x0 -> x2, Pallas kernels: none -> 34.5 us  [the longest x1 33.9 us: shards(): pl.pallas_call(kernel, out_shape=tuple((pltpu.VMEM(shape, F32) for shape...]
  transfers between devices with their start and end apart: 3 -> 0, of which waited for: 3 -> 0; matrix products, arithmetic and copies ran while one was open for 0% -> 0% of each run, Pallas kernels for 0% -> 0%
where the time goes in v1:
time: 35.3 us; the launch traced here: 35.2 us
  Pallas kernels  34.5 us (98%)
  between operations  0.64 us (2%)
    pallas_call x1, Pallas kernels, shards(): pl.pallas_call(kernel, out_shape=tuple((pltpu.VMEM(shape, F32) for shape...  33.9 us

profile of v1, /device:TPU:1, one launch (start us, length us, event | category | flops | bytes accessed | tf_op | source)
XLA Modules:
  0.0 35.2 jit_solution(6689879910194635307)
XLA Ops:
  0.6 33.9 %shard_map.59 = (f32[8,32]{1,0:T(8,128)S(1)}, f32[8,1024]{1,0:T(8,128)S(1)}) custom-call(f32[4,8,256,512]{3,2,1,0:T(8,128)} %bitcast.5, f32[32,512]{1,0:T(8,128)} %bitcast.6, f32[32,64]{1,0:T(8,128)} %bitcast.7, f32[32,128]{1,0:T(8,128)} %bitcast.8), custom_call_target="tpu_custom_call" | custom-call | tf_op jit(solution)/shard_map/pallas_call | solution.py:328
  34.5 0.6 %shard_map.60 = (f32[8,32]{1,0:T(8,128)}, f32[8,1024]{1,0:T(8,128)}) custom-call(f32[8,32]{1,0:T(8,128)S(1)} %get-tuple-element.6.core_in, f32[8,1024]{1,0:T(8,128)S(1)} %get-tuple-element.7.gram_in), custom_call_target="tpu_custom_call" | custom-call | tf_op jit(solution)/shard_map/pallas_call | solution.py:376

commit v2 on v1

v2 whole, which is shorter than its diff:
```python
import functools

import jax
import jax.numpy as jnp
from jax import lax
from jax.experimental import pallas as pl
from jax.experimental.pallas import tpu as pltpu
from jax.sharding import PartitionSpec as P

F32 = jnp.float32
BF16 = jnp.bfloat16
MESH = pl.DeviceIdType.MESH
NN = (((1,), (0,)), ((), ()))
NT = (((1,), (1,)), ((), ()))
RING = (0, 1, 3, 2)
SIZES = (2, 2, 2, 2)
CHUNKS = tuple((sum(SIZES[:c]), SIZES[c]) for c in range(len(SIZES)))
EARLY = 2
ROUNDS = ((0, 3), (3, 1))


def split(values):
    high = values.astype(BF16)
    return high, (values - high.astype(F32)).astype(BF16)


def dot(a, b, dims):
    return lax.dot_general(a, b, dims, preferred_element_type=F32)


def exchange(values, lane, unit, stages):
    for s in stages:
        low = (lane // (unit * s)) % 2 == 0
        out = list(values)
        for a in range(len(values)):
            if a & s:
                continue
            out[a] = jnp.where(low, values[a], pltpu.roll(values[a + s], unit * s, 1))
            out[a + s] = jnp.where(low, pltpu.roll(values[a], 128 - unit * s, 1), values[a + s])
        values = out
    return values


def kernel(
    elev, time_t, north_t, east_t, core_out, gram_out,
    slab, time_v, north_v, basis, send1, recv1, gathered, twin, halves, columns, easts, core_part, core_twin, send2, recv2,
    slab_sem, small_sem, send1_sem, recv1_sem, gather_send, gather_recv, twin_send, twin_recv,
    east_send, east_recv, core_send, core_recv, send2_sem, recv2_sem,
):
    gx, gy, ta = lax.axis_index("gx"), lax.axis_index("gy"), lax.axis_index("ta")
    z, core = gx // 2, gx % 2
    y, x = gy // 2, ta * 2 + gy % 2
    twin_gx = z * 2 + 1 - core

    def slab_copy(c):
        part = pl.ds(*CHUNKS[c])
        return pltpu.make_async_copy(elev.at[:, part], slab.at[:, part], slab_sem.at[c])

    small = [
        pltpu.make_async_copy(time_t, time_v, small_sem.at[0]),
        pltpu.make_async_copy(north_t, north_v, small_sem.at[1]),
        pltpu.make_async_copy(east_t, easts.at[0], small_sem.at[2]),
    ]
    for copy in small:
        copy.start()
    for c in range(2):
        slab_copy(c).start()

    plane, along_x, sheet, across = [], [], [], []
    for slot in range(1, 16):
        y2, x2 = (y + slot // 4) % 4, (x + slot % 4) % 4
        plane.append((slot, (gx, y2 * 2 + x2 % 2, x2 // 2), y2, x2))
    for slot in range(1, 4):
        along_x.append((slot, plane[slot - 1][1], plane[slot - 1][3]))
    for zs in (3, 1, 2, 0):
        for ys in (2, 1, 3, 0):
            if zs or ys:
                y2 = (y + ys) % 4
                sheet.append((zs, (((z + RING[zs]) % 4) * 2 + core, y2 * 2 + gy % 2, ta)))
    for slot in range(4):
        x2 = (x + slot) % 4
        across.append((slot, (twin_gx, y * 2 + x2 % 2, x2 // 2), x2))
    other = across[0][1]
    ring = [(zs, (((z + RING[zs]) % 4) * 2 + core, gy, ta)) for zs in range(1, 4)]
    barrier = pltpu.get_barrier_semaphore()
    peers = [p[1] for p in plane + across] + [device for zs, device in sheet if zs]
    for device in peers:
        pl.semaphore_signal(barrier, inc=1, device_id=device, device_id_type=MESH)

    for copy in small:
        copy.wait()
    time_high, time_low = split(time_v[...])
    time_both = jnp.concatenate([time_high, time_low], 0)
    time_wide = time_high.astype(F32).T.astype(BF16)
    lane64 = lax.broadcasted_iota(jnp.int32, (64, 128), 1)

    def make_basis():
        row = lax.broadcasted_iota(jnp.int32, (32, 128), 0)
        lane = lax.broadcasted_iota(jnp.int32, (32, 128), 1)
        spread = jnp.where(lane // 4 == row, 1.0, 0.0).astype(BF16)
        for h, part in enumerate(split(north_v[...].T)):
            wide = dot(part, spread, NN)
            for x4 in range(4):
                own = jnp.where(lane64 % 4 == x4, wide, 0.0).astype(BF16)
                basis[pl.ds(x4 * 64, 64), pl.ds(h * 128, 128)] = own

    def over_time(g, b):
        high, low = split(slab[b, g])
        t = dot(time_both, high, NT)
        return t[:32] + t[32:] + dot(low, time_wide, NN).T

    def over_y(terms):
        high, low = zip(*[split(t) for t in terms])
        r = dot(jnp.concatenate(high, 0), basis[...], NN)
        return r[:, :128] + r[:, 128:] + dot(jnp.concatenate(low, 0), basis[:, :128], NN)

    def remote(src, dst, send_sem, recv_sem, device):
        return pltpu.make_async_remote_copy(
            src_ref=src, dst_ref=dst, send_sem=send_sem, recv_sem=recv_sem, device_id=device, device_id_type=MESH
        )

    def await_bytes(ref, sem):
        pltpu.make_async_copy(ref, ref, sem).wait()

    def place(qg):
        return (qg % 2) * 2 + qg // 2

    def finish(c, terms):
        start, count = CHUNKS[c]
        for k in range(count):
            sums = over_y(terms[k])
            for b in range(4):
                for qg in range(4):
                    at = b * 32 + qg * 8
                    send1[b, place(qg), start + k] = sums[at : at + 8]
        if c == 0:
            pl.semaphore_wait(barrier, 31)
        part = pl.ds(start, count)
        for slot, device, y2, x2 in plane:
            remote(
                send1.at[y2, x2, part], recv1.at[slot, part], send1_sem.at[c], recv1_sem.at[c], device
            ).start()
        if c == 0:
            for zs, device in ring:
                remote(easts.at[0], easts.at[zs], east_send, east_recv, device).start()

    held = None
    for c, (start, count) in enumerate(CHUNKS):
        slab_copy(c).wait()
        if c + 2 < len(CHUNKS):
            slab_copy(c + 2).start()
        if c > 1:
            finish(c - 1, held)
        held = [[over_time(start + k, b) for b in range(4)] for k in range(count)]
        if c == 0:
            make_basis()
            finish(0, held)
    finish(len(CHUNKS) - 1, held)

    lane8 = lax.broadcasted_iota(jnp.int32, (8, 128), 1)
    own = []
    for c, (start, count) in enumerate(CHUNKS):
        part = pl.ds(start, count)
        await_bytes(recv1.at[pl.ds(1, 15), part], recv1_sem.at[c])
        totals = []
        for g in range(start, start + count):
            total = send1[y, x, g]
            for slot in range(1, 16):
                total = total + recv1[slot, g]
            totals.append(total)
        totals = exchange(totals, lane8, 4, (1,))
        own += totals
        for k in range(count):
            gathered[0, y, start + k] = totals[k]
        for zs, device in sheet:
            remote(
                gathered.at[0, y, part], gathered.at[zs, y, part], gather_send, gather_recv.at[zs, c // EARLY], device
            ).start()
        remote(gathered.at[0, y, part], twin.at[part], twin_send, twin_recv, other).start()

    def left_side(tiles):
        turned = jnp.concatenate(exchange(tiles, lane8, 4, (4, 2)), 0).T
        high, low = split(jnp.concatenate([turned[32 * k : 32 * k + 32] for k in range(4)], 1))
        return jnp.concatenate([high, high, low], 1)

    def half(zs, h):
        by_y = [exchange([gathered[zs, y2, h * 4 + g] for g in range(4)], lane8, 4, (2,)) for y2 in range(4)]
        by_low = [exchange([by_y[y2][k] for y2 in range(4)], lane8, 32, (2, 1)) for k in range(4)]
        return [[by_low[k][high_p] for k in range(4)] for high_p in range(4)]

    def await_half(zs, h):
        ref = gathered.at[0, pl.ds(0, 3), pl.ds(0, 4)] if zs == 0 else gathered.at[zs, :, pl.ds(0, 4)]
        await_bytes(ref, gather_recv.at[zs, h])

    own_left = left_side(own)
    for zs in range(4):
        await_half(zs, 0)
    for zs in range(4):
        tiles = half(zs, 0)
        for high_p in range(4):
            for k in range(4):
                halves[zs, high_p, k] = tiles[high_p][k]
    await_bytes(twin, twin_recv)
    left = jnp.concatenate([own_left, left_side([twin[g] for g in range(8)])], 0)

    for r, (start, count) in enumerate(ROUNDS):
        for zs in range(start, start + count):
            await_half(zs, 1)
        for zs in range(start, start + count):
            second = half(zs, 1)
            tiles = [None] * 32
            for high_p in range(4):
                for k in range(4):
                    pair = exchange([halves[zs, high_p, k], second[high_p][k]], lane8, 16, (1,))
                    tiles[high_p * 8 + k], tiles[high_p * 8 + 4 + k] = pair
            for p in range(32):
                columns[zs, p] = tiles[p]
            high, low = split(jnp.concatenate(tiles, 0))
            product = dot(left, jnp.concatenate([high, low, high], 0), NN)
            for h in range(2):
                for qg in range(4):
                    at = h * 32 + qg * 8
                    send2[h, place(qg), zs] = product[at : at + 8]
        part = pl.ds(start, count)
        for h in range(2):
            for slot, device, at in (along_x, across)[h]:
                remote(
                    send2.at[h, at, part], recv2.at[h, slot, part], send2_sem.at[r, h], recv2_sem.at[r, h], device
                ).start()

    await_bytes(easts.at[pl.ds(1, 3)], east_recv)
    rows = [
        jnp.concatenate([columns[zs, 4 * gx + y], columns[zs, 4 * twin_gx + y]], 0) for zs in range(4)
    ]
    core_sum = lax.dot_general(
        jnp.concatenate(rows, 1),
        jnp.concatenate([easts[zs] for zs in range(4)], 1),
        NT,
        precision=lax.Precision.HIGHEST,
        preferred_element_type=F32,
    )
    core_part[...] = jnp.zeros((8, 128), F32)
    core_part[:, :32] = core_sum[8:]
    core_copy = remote(core_part, core_twin, core_send, core_recv, other)
    core_copy.start()
    core_copy.wait_recv()
    core_out[...] = core_sum[:8] + core_twin[:, :32]

    inverse_count = 1.0 / 1024.0

    def final(zs, c, total):
        at = (((z + 4 - RING[zs]) % 4) * 2 + c) * 128
        gram_out[:, pl.ds(pl.multiple_of(at, 128), 128)] = total * inverse_count

    for r, (start, count) in enumerate(ROUNDS):
        part = pl.ds(start, count)
        await_bytes(recv2.at[0, pl.ds(1, 3), part], recv2_sem.at[r, 0])
        for zs in range(start, start + count):
            total = send2[0, x, zs]
            for slot in range(1, 4):
                total = total + recv2[0, slot, zs]
            final(zs, core, total)
        await_bytes(recv2.at[1, :, part], recv2_sem.at[r, 1])
        for zs in range(start, start + count):
            total = recv2[1, 0, zs]
            for slot in range(1, 4):
                total = total + recv2[1, slot, zs]
            final(zs, 1 - core, total)

    for c, part in enumerate(CHUNKS):
        await_bytes(recv1.at[pl.ds(1, 15), pl.ds(*part)], send1_sem.at[c])
    await_bytes(recv1.at[pl.ds(1, 15)], gather_send)
    await_bytes(twin, twin_send)
    await_bytes(easts.at[pl.ds(1, 3)], east_send)
    core_copy.wait_send()
    for r, part in enumerate(ROUNDS):
        await_bytes(recv2.at[0, pl.ds(1, 3), pl.ds(*part)], send2_sem.at[r, 0])
        await_bytes(recv2.at[1, :, pl.ds(*part)], send2_sem.at[r, 1])


def hand_over(core_in, gram_in, core_out, gram_out, sem):
    copies = [
        pltpu.make_async_copy(core_in, core_out, sem.at[0]),
        pltpu.make_async_copy(gram_in, gram_out, sem.at[1]),
    ]
    for copy in copies:
        copy.start()
    for copy in copies:
        copy.wait()


def shards(elevations, time_basis, north_basis, east_basis):
    dma = pltpu.SemaphoreType.DMA
    shapes = ((8, 32), (8, 1024))
    far = pl.BlockSpec(memory_space=pltpu.HBM)
    near = pl.BlockSpec(memory_space=pltpu.VMEM)
    chunks = len(CHUNKS)
    core_t, gram = pl.pallas_call(
        kernel,
        out_shape=tuple(pltpu.VMEM(shape, F32) for shape in shapes),
        in_specs=[far] * 4,
        out_specs=(near, near),
        scratch_shapes=[
            pltpu.VMEM((4, 8, 256, 512), F32),
            pltpu.VMEM((32, 512), F32),
            pltpu.VMEM((32, 64), F32),
            pltpu.VMEM((256, 256), BF16),
            pltpu.VMEM((4, 4, 8, 8, 128), F32),
            pltpu.VMEM((16, 8, 8, 128), F32),
            pltpu.VMEM((4, 4, 8, 8, 128), F32),
            pltpu.VMEM((8, 8, 128), F32),
            pltpu.VMEM((4, 4, 4, 8, 128), F32),
            pltpu.VMEM((4, 32, 8, 128), F32),
            pltpu.VMEM((4, 32, 128), F32),
            pltpu.VMEM((8, 128), F32),
            pltpu.VMEM((8, 128), F32),
            pltpu.VMEM((2, 4, 4, 8, 128), F32),
            pltpu.VMEM((2, 4, 4, 8, 128), F32),
            dma((chunks,)),
            dma((3,)),
            dma((chunks,)),
            dma((chunks,)),
            dma,
            dma((4, 2)),
            dma,
            dma,
            dma,
            dma,
            dma,
            dma,
            dma((2, 2)),
            dma((2, 2)),
        ],
        compiler_params=pltpu.CompilerParams(
            collective_id=0, has_side_effects=True, vmem_limit_bytes=59 << 20
        ),
    )(elevations.reshape(4, 8, 256, 512), time_basis.T, north_basis.T, east_basis.T)
    core_t, gram = pl.pallas_call(
        hand_over,
        out_shape=tuple(jax.ShapeDtypeStruct(shape, F32) for shape in shapes),
        in_specs=[near, near],
        out_specs=(far, far),
        scratch_shapes=[dma((2,))],
        compiler_params=pltpu.CompilerParams(vmem_limit_bytes=59 << 20),
    )(pltpu.with_memory_space_constraint(core_t, pltpu.VMEM), pltpu.with_memory_space_constraint(gram, pltpu.VMEM))
    return core_t.T, gram


def solution(mesh):
    in_specs = (P("gx", "gy", "ta"), P("ta", None), P("gy", None), P("gx", None))
    out_specs = (P(None, ("gx", "gy", "ta")), P(("gx", "gy", "ta"), None))
    return jax.shard_map(shards, mesh=mesh, in_specs=in_specs, out_specs=out_specs, check_vma=False)
```

time: 35.3 us -> 30.8 us (0.87)
  Pallas kernels: 34.5 us -> 30.1 us
    pallas_call x1, Pallas kernels: 33.9 us -> 29.4 us  [shards(): pl.pallas_call(kernel, out_shape=tuple((pltpu.VMEM(shape, F32) for shape...]
where the time goes in v2:
time: 30.8 us; the launch traced here: 30.7 us
  Pallas kernels  30.1 us (98%)
  between operations  0.64 us (2%)
    pallas_call x1, Pallas kernels, shards(): pl.pallas_call(kernel, out_shape=tuple((pltpu.VMEM(shape, F32) for shape...  29.4 us
    pallas_call x1, Pallas kernels, shards(): pl.pallas_call(hand_over, out_shape=tuple((jax.ShapeDtypeStruct(shape, F3...  0.64 us

profile of v2, /device:TPU:1, one launch (start us, length us, event | category | flops | bytes accessed | tf_op | source)
XLA Modules:
  0.0 30.7 jit_solution(4843662602578518809)
XLA Ops:
  0.6 29.4 %shard_map.59 = (f32[8,32]{1,0:T(8,128)S(1)}, f32[8,1024]{1,0:T(8,128)S(1)}) custom-call(f32[4,8,256,512]{3,2,1,0:T(8,128)} %bitcast.5, f32[32,512]{1,0:T(8,128)} %bitcast.6, f32[32,64]{1,0:T(8,128)} %bitcast.7, f32[32,128]{1,0:T(8,128)} %bitcast.8), custom_call_target="tpu_custom_call" | custom-call | tf_op jit(solution)/shard_map/pallas_call | solution.py:298
  30.1 0.6 %shard_map.60 = (f32[8,32]{1,0:T(8,128)}, f32[8,1024]{1,0:T(8,128)}) custom-call(f32[8,32]{1,0:T(8,128)S(1)} %get-tuple-element.6.core_in, f32[8,1024]{1,0:T(8,128)S(1)} %get-tuple-element.7.gram_in), custom_call_target="tpu_custom_call" | custom-call | tf_op jit(solution)/shard_map/pallas_call | solution.py:338

commit v3 on v2

--- a/solution.py
+++ b/solution.py
@@ -12,11 +12,10 @@
 MESH = pl.DeviceIdType.MESH
 NN = (((1,), (0,)), ((), ()))
 NT = (((1,), (1,)), ((), ()))
-RING = (0, 1, 3, 2)
 SIZES = (2, 2, 2, 2)
 CHUNKS = tuple((sum(SIZES[:c]), SIZES[c]) for c in range(len(SIZES)))
 EARLY = 2
-ROUNDS = ((0, 3), (3, 1))
+ROUNDS = ((0, 1), (1, 1))
 
 
 def split(values):
@@ -43,14 +42,14 @@
 
 def kernel(
     elev, time_t, north_t, east_t, core_out, gram_out,
-    slab, time_v, north_v, basis, send1, recv1, gathered, twin, halves, columns, easts, core_part, core_twin, send2, recv2,
-    slab_sem, small_sem, send1_sem, recv1_sem, gather_send, gather_recv, twin_send, twin_recv,
+    slab, time_v, north_v, basis, send1, recv1, gathered, mate_tiles, halves, columns, easts, core_part, core_mates, send2, recv2,
+    slab_sem, small_sem, send1_sem, recv1_sem, gather_send, gather_recv, mate_send, mate_recv,
     east_send, east_recv, core_send, core_recv, send2_sem, recv2_sem,
 ):
     gx, gy, ta = lax.axis_index("gx"), lax.axis_index("gy"), lax.axis_index("ta")
     z, core = gx // 2, gx % 2
     y, x = gy // 2, ta * 2 + gy % 2
-    twin_gx = z * 2 + 1 - core
+    mates = [z2 * 2 + c2 for z2 in (z, z + 1 - 2 * (z % 2)) for c2 in (core, 1 - core)]
 
     def slab_copy(c):
         part = pl.ds(*CHUNKS[c])
@@ -66,22 +65,23 @@
     for c in range(2):
         slab_copy(c).start()
 
-    plane, along_x, sheet, across = [], [], [], []
+    plane, sheet = [], []
     for slot in range(1, 16):
         y2, x2 = (y + slot // 4) % 4, (x + slot % 4) % 4
         plane.append((slot, (gx, y2 * 2 + x2 % 2, x2 // 2), y2, x2))
-    for slot in range(1, 4):
-        along_x.append((slot, plane[slot - 1][1], plane[slot - 1][3]))
-    for zs in (3, 1, 2, 0):
+    for zs in (1, 0):
         for ys in (2, 1, 3, 0):
             if zs or ys:
                 y2 = (y + ys) % 4
-                sheet.append((zs, (((z + RING[zs]) % 4) * 2 + core, y2 * 2 + gy % 2, ta)))
-    for slot in range(4):
-        x2 = (x + slot) % 4
-        across.append((slot, (twin_gx, y * 2 + x2 % 2, x2 // 2), x2))
-    other = across[0][1]
-    ring = [(zs, (((z + RING[zs]) % 4) * 2 + core, gy, ta)) for zs in range(1, 4)]
+                sheet.append((zs, ((gx + 4 * zs) % 8, y2 * 2 + gy % 2, ta)))
+    rings = []
+    for m in range(4):
+        ring = []
+        for slot in range(4):
+            x2 = (x + slot) % 4
+            ring.append((slot, (mates[m], y * 2 + x2 % 2, x2 // 2), x2))
+        rings.append(ring if m else ring[1:])
+    across = rings[1] + rings[2] + rings[3]
     barrier = pltpu.get_barrier_semaphore()
     peers = [p[1] for p in plane + across] + [device for zs, device in sheet if zs]
     for device in peers:
@@ -141,8 +141,8 @@
                 send1.at[y2, x2, part], recv1.at[slot, part], send1_sem.at[c], recv1_sem.at[c], device
             ).start()
         if c == 0:
-            for zs, device in ring:
-                remote(easts.at[0], easts.at[zs], east_send, east_recv, device).start()
+            for zs, device in sheet[3:4]:
+                remote(easts.at[0], easts.at[1], east_send, east_recv, device).start()
 
     held = None
     for c, (start, count) in enumerate(CHUNKS):
@@ -176,7 +176,8 @@
             remote(
                 gathered.at[0, y, part], gathered.at[zs, y, part], gather_send, gather_recv.at[zs, c // EARLY], device
             ).start()
-        remote(gathered.at[0, y, part], twin.at[part], twin_send, twin_recv, other).start()
+        for m in range(1, 4):
+            remote(gathered.at[0, y, part], mate_tiles.at[m - 1, part], mate_send, mate_recv, rings[m][0][1]).start()
 
     def left_side(tiles):
         turned = jnp.concatenate(exchange(tiles, lane8, 4, (4, 2)), 0).T
@@ -192,16 +193,18 @@
         ref = gathered.at[0, pl.ds(0, 3), pl.ds(0, 4)] if zs == 0 else gathered.at[zs, :, pl.ds(0, 4)]
         await_bytes(ref, gather_recv.at[zs, h])
 
-    own_left = left_side(own)
-    for zs in range(4):
+    lefts = [left_side(own)]
+    for zs in range(2):
         await_half(zs, 0)
-    for zs in range(4):
+    for zs in range(2):
         tiles = half(zs, 0)
         for high_p in range(4):
             for k in range(4):
                 halves[zs, high_p, k] = tiles[high_p][k]
-    await_bytes(twin, twin_recv)
-    left = jnp.concatenate([own_left, left_side([twin[g] for g in range(8)])], 0)
+    await_bytes(mate_tiles, mate_recv)
+    for m in range(3):
+        lefts.append(left_side([mate_tiles[m, g] for g in range(8)]))
+    left = jnp.concatenate(lefts, 0)
 
     for r, (start, count) in enumerate(ROUNDS):
         for zs in range(start, start + count):
@@ -217,65 +220,66 @@
                 columns[zs, p] = tiles[p]
             high, low = split(jnp.concatenate(tiles, 0))
             product = dot(left, jnp.concatenate([high, low, high], 0), NN)
-            for h in range(2):
+            for m in range(4):
                 for qg in range(4):
-                    at = h * 32 + qg * 8
-                    send2[h, place(qg), zs] = product[at : at + 8]
+                    at = m * 32 + qg * 8
+                    send2[m, place(qg), zs] = product[at : at + 8]
         part = pl.ds(start, count)
-        for h in range(2):
-            for slot, device, at in (along_x, across)[h]:
+        for m in (3, 2, 1, 0):
+            for slot, device, at in rings[m]:
                 remote(
-                    send2.at[h, at, part], recv2.at[h, slot, part], send2_sem.at[r, h], recv2_sem.at[r, h], device
+                    send2.at[m, at, part], recv2.at[m, slot, part], send2_sem.at[r, m], recv2_sem.at[r, m], device
                 ).start()
 
-    await_bytes(easts.at[pl.ds(1, 3)], east_recv)
-    rows = [
-        jnp.concatenate([columns[zs, 4 * gx + y], columns[zs, 4 * twin_gx + y]], 0) for zs in range(4)
-    ]
+    await_bytes(easts.at[1], east_recv)
+    rows = [jnp.concatenate([columns[zs, 4 * mates[m] + y] for m in range(4)], 0) for zs in range(2)]
     core_sum = lax.dot_general(
         jnp.concatenate(rows, 1),
-        jnp.concatenate([easts[zs] for zs in range(4)], 1),
+        jnp.concatenate([easts[zs] for zs in range(2)], 1),
         NT,
         precision=lax.Precision.HIGHEST,
         preferred_element_type=F32,
     )
-    core_part[...] = jnp.zeros((8, 128), F32)
-    core_part[:, :32] = core_sum[8:]
-    core_copy = remote(core_part, core_twin, core_send, core_recv, other)
-    core_copy.start()
-    core_copy.wait_recv()
-    core_out[...] = core_sum[:8] + core_twin[:, :32]
+    core_part[...] = jnp.zeros((3, 8, 128), F32)
+    core_copies = []
+    for m in range(1, 4):
+        core_part[m - 1, :, :32] = core_sum[8 * m : 8 * m + 8]
+        core_copies.append(
+            remote(core_part.at[m - 1], core_mates.at[m - 1], core_send.at[m - 1], core_recv.at[m - 1], rings[m][0][1])
+        )
+    for copy in core_copies:
+        copy.start()
+    total = core_sum[:8]
+    for m in range(3):
+        core_copies[m].wait_recv()
+        total = total + core_mates[m, :, :32]
+    core_out[...] = total
 
     inverse_count = 1.0 / 1024.0
-
-    def final(zs, c, total):
-        at = (((z + 4 - RING[zs]) % 4) * 2 + c) * 128
-        gram_out[:, pl.ds(pl.multiple_of(at, 128), 128)] = total * inverse_count
 
     for r, (start, count) in enumerate(ROUNDS):
         part = pl.ds(start, count)
-        await_bytes(recv2.at[0, pl.ds(1, 3), part], recv2_sem.at[r, 0])
-        for zs in range(start, start + count):
-            total = send2[0, x, zs]
-            for slot in range(1, 4):
-                total = total + recv2[0, slot, zs]
-            final(zs, core, total)
-        await_bytes(recv2.at[1, :, part], recv2_sem.at[r, 1])
-        for zs in range(start, start + count):
-            total = recv2[1, 0, zs]
-            for slot in range(1, 4):
-                total = total + recv2[1, slot, zs]
-            final(zs, 1 - core, total)
+        for m in range(4):
+            peers = range(4) if m else range(1, 4)
+            await_bytes(recv2.at[m, pl.ds(peers[0], len(peers)), part], recv2_sem.at[r, m])
+            for zs in range(start, start + count):
+                total = recv2[m, 0, zs] if m else send2[0, x, zs]
+                for slot in range(1, 4):
+                    total = total + recv2[m, slot, zs]
+                at = ((mates[m] + 4 * zs) % 8) * 128
+                gram_out[:, pl.ds(pl.multiple_of(at, 128), 128)] = total * inverse_count
 
     for c, part in enumerate(CHUNKS):
         await_bytes(recv1.at[pl.ds(1, 15), pl.ds(*part)], send1_sem.at[c])
-    await_bytes(recv1.at[pl.ds(1, 15)], gather_send)
-    await_bytes(twin, twin_send)
-    await_bytes(easts.at[pl.ds(1, 3)], east_send)
-    core_copy.wait_send()
+    await_bytes(recv1.at[pl.ds(1, 7)], gather_send)
+    await_bytes(mate_tiles, mate_send)
+    await_bytes(easts.at[1], east_send)
+    for copy in core_copies:
+        copy.wait_send()
     for r, part in enumerate(ROUNDS):
-        await_bytes(recv2.at[0, pl.ds(1, 3), pl.ds(*part)], send2_sem.at[r, 0])
-        await_bytes(recv2.at[1, :, pl.ds(*part)], send2_sem.at[r, 1])
+        for m in range(4):
+            peers = range(4) if m else range(1, 4)
+            await_bytes(recv2.at[m, pl.ds(peers[0], len(peers)), pl.ds(*part)], send2_sem.at[r, m])
 
 
 def hand_over(core_in, gram_in, core_out, gram_out, sem):
@@ -307,29 +311,29 @@
             pltpu.VMEM((256, 256), BF16),
             pltpu.VMEM((4, 4, 8, 8, 128), F32),
             pltpu.VMEM((16, 8, 8, 128), F32),
-            pltpu.VMEM((4, 4, 8, 8, 128), F32),
-            pltpu.VMEM((8, 8, 128), F32),
-            pltpu.VMEM((4, 4, 4, 8, 128), F32),
-            pltpu.VMEM((4, 32, 8, 128), F32),
-            pltpu.VMEM((4, 32, 128), F32),
-            pltpu.VMEM((8, 128), F32),
-            pltpu.VMEM((8, 128), F32),
+            pltpu.VMEM((2, 4, 8, 8, 128), F32),
+            pltpu.VMEM((3, 8, 8, 128), F32),
             pltpu.VMEM((2, 4, 4, 8, 128), F32),
-            pltpu.VMEM((2, 4, 4, 8, 128), F32),
+            pltpu.VMEM((2, 32, 8, 128), F32),
+            pltpu.VMEM((2, 32, 128), F32),
+            pltpu.VMEM((3, 8, 128), F32),
+            pltpu.VMEM((3, 8, 128), F32),
+            pltpu.VMEM((4, 4, 2, 8, 128), F32),
+            pltpu.VMEM((4, 4, 2, 8, 128), F32),
             dma((chunks,)),
             dma((3,)),
             dma((chunks,)),
             dma((chunks,)),
             dma,
-            dma((4, 2)),
-            dma,
-            dma,
-            dma,
-            dma,
-            dma,
-            dma,
             dma((2, 2)),
-            dma((2, 2)),
+            dma,
+            dma,
+            dma,
+            dma,
+            dma((3,)),
+            dma((3,)),
+            dma((2, 4)),
+            dma((2, 4)),
         ],
         compiler_params=pltpu.CompilerParams(
             collective_id=0, has_side_effects=True, vmem_limit_bytes=59 << 20

time: 30.8 us -> 29 us (0.942)
  Pallas kernels: 30.1 us -> 28.3 us
    pallas_call x1, Pallas kernels: 29.4 us -> 27.6 us  [shards(): pl.pallas_call(kernel, out_shape=tuple((pltpu.VMEM(shape, F32) for shape...]
where the time goes in v3:
time: 29 us; the launch traced here: 28.9 us
  Pallas kernels  28.3 us (98%)
  between operations  0.64 us (2%)
    pallas_call x1, Pallas kernels, shards(): pl.pallas_call(kernel, out_shape=tuple((pltpu.VMEM(shape, F32) for shape...  27.6 us
    pallas_call x1, Pallas kernels, shards(): pl.pallas_call(hand_over, out_shape=tuple((jax.ShapeDtypeStruct(shape, F3...  0.64 us

profile of v3, /device:TPU:1, one launch (start us, length us, event | category | flops | bytes accessed | tf_op | source)
XLA Modules:
  0.0 28.9 jit_solution(16111292924373122176)
XLA Ops:
  0.6 27.6 %shard_map.59 = (f32[8,32]{1,0:T(8,128)S(1)}, f32[8,1024]{1,0:T(8,128)S(1)}) custom-call(f32[4,8,256,512]{3,2,1,0:T(8,128)} %bitcast.5, f32[32,512]{1,0:T(8,128)} %bitcast.6, f32[32,64]{1,0:T(8,128)} %bitcast.7, f32[32,128]{1,0:T(8,128)} %bitcast.8), custom_call_target="tpu_custom_call" | custom-call | tf_op jit(solution)/shard_map/pallas_call | solution.py:302
  28.3 0.6 %shard_map.60 = (f32[8,32]{1,0:T(8,128)}, f32[8,1024]{1,0:T(8,128)}) custom-call(f32[8,32]{1,0:T(8,128)S(1)} %get-tuple-element.6.core_in, f32[8,1024]{1,0:T(8,128)S(1)} %get-tuple-element.7.gram_in), custom_call_target="tpu_custom_call" | custom-call | tf_op jit(solution)/shard_map/pallas_call | solution.py:342

commit v4 on v3

--- a/solution.py
+++ b/solution.py
@@ -49,7 +49,9 @@
     gx, gy, ta = lax.axis_index("gx"), lax.axis_index("gy"), lax.axis_index("ta")
     z, core = gx // 2, gx % 2
     y, x = gy // 2, ta * 2 + gy % 2
-    mates = [z2 * 2 + c2 for z2 in (z, z + 1 - 2 * (z % 2)) for c2 in (core, 1 - core)]
+    near, beyond = z + 1 - 2 * (z % 2), (z + 3 + 2 * (z % 2)) % 4
+    mates = [z2 * 2 + c2 for z2 in (z, near) for c2 in (core, 1 - core)]
+    gathered_by = [(z2 * 2 + c2, z3 * 2 + c2) for z2, z3 in ((z, beyond), (near, (z + 2) % 4)) for c2 in (core, 1 - core)]
 
     def slab_copy(c):
         part = pl.ds(*CHUNKS[c])
@@ -73,7 +75,7 @@
         for ys in (2, 1, 3, 0):
             if zs or ys:
                 y2 = (y + ys) % 4
-                sheet.append((zs, ((gx + 4 * zs) % 8, y2 * 2 + gy % 2, ta)))
+                sheet.append((zs, (gathered_by[0][zs], y2 * 2 + gy % 2, ta)))
     rings = []
     for m in range(4):
         ring = []
@@ -266,7 +268,7 @@
                 total = recv2[m, 0, zs] if m else send2[0, x, zs]
                 for slot in range(1, 4):
                     total = total + recv2[m, slot, zs]
-                at = ((mates[m] + 4 * zs) % 8) * 128
+                at = gathered_by[m][zs] * 128
                 gram_out[:, pl.ds(pl.multiple_of(at, 128), 128)] = total * inverse_count
 
     for c, part in enumerate(CHUNKS):

time: 29 us -> 28.9 us (level)
  no operation moved by 1% of the time
where the time goes in v4:
time: 28.9 us; the launch traced here: 28.8 us
  Pallas kernels  28.1 us (97%)
  between operations  0.64 us (2%)
    pallas_call x1, Pallas kernels, shards(): pl.pallas_call(kernel, out_shape=tuple((pltpu.VMEM(shape, F32) for shape...  27.5 us
    pallas_call x1, Pallas kernels, shards(): pl.pallas_call(hand_over, out_shape=tuple((jax.ShapeDtypeStruct(shape, F3...  0.64 us

profile of v4, /device:TPU:1, one launch (start us, length us, event | category | flops | bytes accessed | tf_op | source)
XLA Modules:
  0.0 28.8 jit_solution(17519548156599868525)
XLA Ops:
  0.6 27.5 %shard_map.59 = (f32[8,32]{1,0:T(8,128)S(1)}, f32[8,1024]{1,0:T(8,128)S(1)}) custom-call(f32[4,8,256,512]{3,2,1,0:T(8,128)} %bitcast.5, f32[32,512]{1,0:T(8,128)} %bitcast.6, f32[32,64]{1,0:T(8,128)} %bitcast.7, f32[32,128]{1,0:T(8,128)} %bitcast.8), custom_call_target="tpu_custom_call" | custom-call | tf_op jit(solution)/shard_map/pallas_call | solution.py:304
  28.1 0.6 %shard_map.60 = (f32[8,32]{1,0:T(8,128)}, f32[8,1024]{1,0:T(8,128)}) custom-call(f32[8,32]{1,0:T(8,128)S(1)} %get-tuple-element.6.core_in, f32[8,1024]{1,0:T(8,128)S(1)} %get-tuple-element.7.gram_in), custom_call_target="tpu_custom_call" | custom-call | tf_op jit(solution)/shard_map/pallas_call | solution.py:344

commit v5 on v4

--- a/solution.py
+++ b/solution.py
@@ -79,11 +79,12 @@
     rings = []
     for m in range(4):
         ring = []
-        for slot in range(4):
+        for slot in (2, 1, 3, 0):
             x2 = (x + slot) % 4
             ring.append((slot, (mates[m], y * 2 + x2 % 2, x2 // 2), x2))
-        rings.append(ring if m else ring[1:])
+        rings.append(ring if m else ring[:3])
     across = rings[1] + rings[2] + rings[3]
+    far_first = sorted(plane, key=lambda p: -((0, 1, 2, 1)[p[0] // 4] + (0, 1, 2, 1)[p[0] % 4]))
     barrier = pltpu.get_barrier_semaphore()
     peers = [p[1] for p in plane + across] + [device for zs, device in sheet if zs]
     for device in peers:
@@ -138,7 +139,7 @@
         if c == 0:
             pl.semaphore_wait(barrier, 31)
         part = pl.ds(start, count)
-        for slot, device, y2, x2 in plane:
+        for slot, device, y2, x2 in far_first:
             remote(
                 send1.at[y2, x2, part], recv1.at[slot, part], send1_sem.at[c], recv1_sem.at[c], device
             ).start()
@@ -146,18 +147,12 @@
             for zs, device in sheet[3:4]:
                 remote(easts.at[0], easts.at[1], east_send, east_recv, device).start()
 
-    held = None
+    make_basis()
     for c, (start, count) in enumerate(CHUNKS):
         slab_copy(c).wait()
         if c + 2 < len(CHUNKS):
             slab_copy(c + 2).start()
-        if c > 1:
-            finish(c - 1, held)
-        held = [[over_time(start + k, b) for b in range(4)] for k in range(count)]
-        if c == 0:
-            make_basis()
-            finish(0, held)
-    finish(len(CHUNKS) - 1, held)
+        finish(c, [[over_time(start + k, b) for b in range(4)] for k in range(count)])
 
     lane8 = lax.broadcasted_iota(jnp.int32, (8, 128), 1)
     own = []
@@ -179,7 +174,7 @@
                 gathered.at[0, y, part], gathered.at[zs, y, part], gather_send, gather_recv.at[zs, c // EARLY], device
             ).start()
         for m in range(1, 4):
-            remote(gathered.at[0, y, part], mate_tiles.at[m - 1, part], mate_send, mate_recv, rings[m][0][1]).start()
+            remote(gathered.at[0, y, part], mate_tiles.at[m - 1, part], mate_send, mate_recv, rings[m][3][1]).start()
 
     def left_side(tiles):
         turned = jnp.concatenate(exchange(tiles, lane8, 4, (4, 2)), 0).T
@@ -247,7 +242,7 @@
     for m in range(1, 4):
         core_part[m - 1, :, :32] = core_sum[8 * m : 8 * m + 8]
         core_copies.append(
-            remote(core_part.at[m - 1], core_mates.at[m - 1], core_send.at[m - 1], core_recv.at[m - 1], rings[m][0][1])
+            remote(core_part.at[m - 1], core_mates.at[m - 1], core_send.at[m - 1], core_recv.at[m - 1], rings[m][3][1])
         )
     for copy in core_copies:
         copy.start()

time: 28.9 us -> 28.5 us (0.986)
  Pallas kernels: 28.1 us -> 27.8 us
    pallas_call x1, Pallas kernels: 27.5 us -> 27.2 us  [shards(): pl.pallas_call(kernel, out_shape=tuple((pltpu.VMEM(shape, F32) for shape...]
where the time goes in v5:
time: 28.5 us; the launch traced here: 28.4 us
  Pallas kernels  27.8 us (98%)
  between operations  0.64 us (2%)
    pallas_call x1, Pallas kernels, shards(): pl.pallas_call(kernel, out_shape=tuple((pltpu.VMEM(shape, F32) for shape...  27.2 us
    pallas_call x1, Pallas kernels, shards(): pl.pallas_call(hand_over, out_shape=tuple((jax.ShapeDtypeStruct(shape, F3...  0.64 us

profile of v5, /device:TPU:1, one launch (start us, length us, event | category | flops | bytes accessed | tf_op | source)
XLA Modules:
  0.0 28.4 jit_solution(7262471318880560336)
XLA Ops:
  0.6 27.2 %shard_map.59 = (f32[8,32]{1,0:T(8,128)S(1)}, f32[8,1024]{1,0:T(8,128)S(1)}) custom-call(f32[4,8,256,512]{3,2,1,0:T(8,128)} %bitcast.5, f32[32,512]{1,0:T(8,128)} %bitcast.6, f32[32,64]{1,0:T(8,128)} %bitcast.7, f32[32,128]{1,0:T(8,128)} %bitcast.8), custom_call_target="tpu_custom_call" | custom-call | tf_op jit(solution)/shard_map/pallas_call | solution.py:299
  27.8 0.6 %shard_map.60 = (f32[8,32]{1,0:T(8,128)}, f32[8,1024]{1,0:T(8,128)}) custom-call(f32[8,32]{1,0:T(8,128)S(1)} %get-tuple-element.6.core_in, f32[8,1024]{1,0:T(8,128)S(1)} %get-tuple-element.7.gram_in), custom_call_target="tpu_custom_call" | custom-call | tf_op jit(solution)/shard_map/pallas_call | solution.py:339

commit v6 on v5

--- a/solution.py
+++ b/solution.py
@@ -14,6 +14,7 @@
 NT = (((1,), (1,)), ((), ()))
 SIZES = (2, 2, 2, 2)
 CHUNKS = tuple((sum(SIZES[:c]), SIZES[c]) for c in range(len(SIZES)))
+LAST = len(CHUNKS) - 1
 EARLY = 2
 ROUNDS = ((0, 1), (1, 1))
 
@@ -54,8 +55,11 @@
     gathered_by = [(z2 * 2 + c2, z3 * 2 + c2) for z2, z3 in ((z, beyond), (near, (z + 2) % 4)) for c2 in (core, 1 - core)]
 
     def slab_copy(c):
-        part = pl.ds(*CHUNKS[c])
-        return pltpu.make_async_copy(elev.at[:, part], slab.at[:, part], slab_sem.at[c])
+        if c < LAST:
+            part = pl.ds(*CHUNKS[c])
+            return pltpu.make_async_copy(elev.at[:, part], slab.at[:, part], slab_sem.at[c])
+        part, times = pl.ds(*CHUNKS[LAST]), pl.ds((c - LAST) * 256, 256)
+        return pltpu.make_async_copy(elev.at[:, part, :, times], slab.at[:, part, :, times], slab_sem.at[c])
 
     small = [
         pltpu.make_async_copy(time_t, time_v, small_sem.at[0]),
@@ -107,10 +111,10 @@
                 own = jnp.where(lane64 % 4 == x4, wide, 0.0).astype(BF16)
                 basis[pl.ds(x4 * 64, 64), pl.ds(h * 128, 128)] = own
 
-    def over_time(g, b):
-        high, low = split(slab[b, g])
-        t = dot(time_both, high, NT)
-        return t[:32] + t[32:] + dot(low, time_wide, NN).T
+    def over_time(g, b, first=0, last=512):
+        high, low = split(slab[b, g, :, first:last])
+        t = dot(time_both[:, first:last], high, NT)
+        return t[:32] + t[32:] + dot(low, time_wide[first:last], NN).T
 
     def over_y(terms):
         high, low = zip(*[split(t) for t in terms])
@@ -150,9 +154,14 @@
     make_basis()
     for c, (start, count) in enumerate(CHUNKS):
         slab_copy(c).wait()
-        if c + 2 < len(CHUNKS):
+        if c + 2 <= LAST + 1:
             slab_copy(c + 2).start()
-        finish(c, [[over_time(start + k, b) for b in range(4)] for k in range(count)])
+        if c < LAST:
+            finish(c, [[over_time(start + k, b) for b in range(4)] for k in range(count)])
+    start, count = CHUNKS[LAST]
+    early = [[over_time(start + k, b, 0, 256) for b in range(4)] for k in range(count)]
+    slab_copy(LAST + 1).wait()
+    finish(LAST, [[early[k][b] + over_time(start + k, b, 256, 512) for b in range(4)] for k in range(count)])
 
     lane8 = lax.broadcasted_iota(jnp.int32, (8, 128), 1)
     own = []
@@ -317,7 +326,7 @@
             pltpu.VMEM((3, 8, 128), F32),
             pltpu.VMEM((4, 4, 2, 8, 128), F32),
             pltpu.VMEM((4, 4, 2, 8, 128), F32),
-            dma((chunks,)),
+            dma((chunks + 1,)),
             dma((3,)),
             dma((chunks,)),
             dma((chunks,)),

time: 28.5 us -> 28.6 us (level)
  no operation moved by 1% of the time
where the time goes in v6:
time: 28.6 us; the launch traced here: 28.4 us
  Pallas kernels  27.8 us (97%)
  between operations  0.64 us (2%)
    pallas_call x1, Pallas kernels, shards(): pl.pallas_call(kernel, out_shape=tuple((pltpu.VMEM(shape, F32) for shape...  27.2 us
    pallas_call x1, Pallas kernels, shards(): pl.pallas_call(hand_over, out_shape=tuple((jax.ShapeDtypeStruct(shape, F3...  0.64 us

profile of v6, /device:TPU:1, one launch (start us, length us, event | category | flops | bytes accessed | tf_op | source)
XLA Modules:
  0.0 28.4 jit_solution(8534181367569467679)
XLA Ops:
  0.6 27.2 %shard_map.59 = (f32[8,32]{1,0:T(8,128)S(1)}, f32[8,1024]{1,0:T(8,128)S(1)}) custom-call(f32[4,8,256,512]{3,2,1,0:T(8,128)} %bitcast.5, f32[32,512]{1,0:T(8,128)} %bitcast.6, f32[32,64]{1,0:T(8,128)} %bitcast.7, f32[32,128]{1,0:T(8,128)} %bitcast.8), custom_call_target="tpu_custom_call" | custom-call | tf_op jit(solution)/shard_map/pallas_call | solution.py:308
  27.8 0.6 %shard_map.60 = (f32[8,32]{1,0:T(8,128)}, f32[8,1024]{1,0:T(8,128)}) custom-call(f32[8,32]{1,0:T(8,128)S(1)} %get-tuple-element.6.core_in, f32[8,1024]{1,0:T(8,128)S(1)} %get-tuple-element.7.gram_in), custom_call_target="tpu_custom_call" | custom-call | tf_op jit(solution)/shard_map/pallas_call | solution.py:348
